TPU v7x, 256 devices: a whole 4x4x8 slice. The times are simulated.
256 devices in a mesh: freq: 16 (over y_hi, x, core), recv: 16 (over y_lo, z).
Axes of the slice: x: 4, y: 4 (y_hi: 2, y_lo: 2; y = y_hi * 2 + y_lo), z: 8, core: 2. Of those that a mesh axis runs over, the one named last changes fastest.
Arguments:
- response: bfloat16 [2, 256, 512, 4096], P(None, 'freq', 'recv'), may hold values from -0.0625 to 0.0625
- focusing: float32 [2, 256, 16, 4096], P(None, 'freq', None, 'recv'), may hold values from -6 to 6
- window_onset: int32 [16, 512], P(None, ('recv', 'freq')), may hold values from 0 to 511
- window_end: int32 [16, 512], P(None, ('recv', 'freq')), may hold values from 128 to 1023, as said below
Outputs:
- windowed: float32 [16, 512, 1024], P(None, ('recv', 'freq'))
Inputs may be any that keep to these rules, and one draw needn't show every extreme that they name: window_end - window_onset lies between 128 and 512 for every trace.
All inputs are finite; a program needn't handle non-finite values.
Results may differ from a plain program's by a relative error of at most 0.0029.
Values may be sent and summed in bfloat16 or wider, within the bound.
No kernel may reach another device: no remote copies, remote signals or barrier semaphores. Data moves between devices by JAX's collectives and lax.ppermute only.
A program may use at most 64 MiB of HBM per device.

v0:
```python
import math
import jax
import jax.numpy as jnp
from jax import lax
from jax.sharding import PartitionSpec as P

NF = 256
NT = 1024


def make_table(count):
    freqs = jnp.arange(count, dtype=jnp.int32)
    samples = jnp.arange(NT, dtype=jnp.int32)
    phase = (freqs[:, None] * samples[None, :] % NT).astype(jnp.float32) * (2.0 * math.pi / NT)
    scale = 1.0 / math.sqrt(NF)
    return jnp.concatenate([jnp.cos(phase) * scale, -jnp.sin(phase) * scale], 0)


def transform(stacked, table):
    return lax.dot_general(
        stacked,
        table,
        (((0,), (0,)), ((), ())),
        precision=lax.Precision.HIGHEST,
        preferred_element_type=jnp.float32,
    )


def per_device(response, focusing, window_onset, window_end):
    focal = focusing.shape[2]
    focus_half = focusing.astype(jnp.bfloat16)
    gathered = lax.all_gather(focus_half, "recv", axis=3, tiled=True)
    real_part = jnp.einsum(
        "krs,kqs->krq", response[0], gathered[0], preferred_element_type=jnp.float32
    )
    real_part = real_part - jnp.einsum(
        "krs,kqs->krq", response[1], gathered[1], preferred_element_type=jnp.float32
    )
    imag_part = jnp.einsum(
        "krs,kqs->krq", response[0], gathered[1], preferred_element_type=jnp.float32
    )
    imag_part = imag_part + jnp.einsum(
        "krs,kqs->krq", response[1], gathered[0], preferred_element_type=jnp.float32
    )
    spectra = jnp.stack([real_part, imag_part])
    owned = window_onset.shape[1]
    moved = lax.all_to_all(spectra, "freq", split_axis=2, concat_axis=1, tiled=True)
    flat = moved.reshape(2 * NF, owned * focal)
    traces = transform(flat, make_table(NF))
    traces = jnp.transpose(traces.reshape(owned, focal, NT), (1, 0, 2))
    samples = jnp.arange(NT, dtype=jnp.int32)
    keep = (samples[None, None, :] >= window_onset[:, :, None]) & (
        samples[None, None, :] < window_end[:, :, None]
    )
    return jnp.where(keep, traces, jnp.float32(0.0))


def solution(mesh):
    in_specs = (
        P(None, "freq", "recv", None),
        P(None, "freq", None, "recv"),
        P(None, ("recv", "freq")),
        P(None, ("recv", "freq")),
    )
    out_specs = P(None, ("recv", "freq"), None)
    return jax.shard_map(
        per_device, mesh=mesh, in_specs=in_specs, out_specs=out_specs, check_vma=False
    )
```

profile of v0, /device:TPU:1, one launch (start us, length us, event | category | flops | bytes accessed | tf_op | source)
XLA Modules:
  0.0 139.6 jit_solution(12699561626764175694)
XLA Ops:
  6.5 0.0 all-gather.2.cloned.1.call-start
  6.5 1.8 %convert_element_type.8 = bf16[2,16,16,256]{3,2,1,0:T(8,128)(2,1)} convert(f32[2,16,16,256]{3,2,1,0:T(8,128)} %param.5) | non-fusion elementwise | flops 131072 | bytes 786432 | tf_op jit(solution)/shard_map/convert_element_type | solution.py:31
  8.3 0.0 all-gather.2.cloned.1.call-update
  8.3 84.3 %all-gather.2.cloned.1.call-done = bf16[2,16,16,4096]{3,2,1,0:T(8,128)(2,1)} async-done(((bf16[2,16,16,256]{3,2,1,0:T(8,128)(2,1)}), bf16[2,16,16,4096]{3,2,1,0:T(8,128)(2,1)}) %all-gather.2.cloned.1.call-update) | async-done | bytes 4194320 | tf_op jit(solution)/shard_map/all_gather | solution.py:32
  92.7 0.0 copy-start.2
  92.7 4.2 %fusion.2 = f32[16,32,16]{1,2,0:T(8,128)S(1)} fusion(bf16[2,16,32,4096]{3,2,1,0:T(8,128)(2,1)} %param.4, bf16[2,16,16,4096]{3,2,1,0:T(8,128)(2,1)} %all-gather.2.cloned.1.call-done), kind=kOutput, calls=%fused_computation.2 | convolution fusion | flops 67108864 | bytes 6324224 | tf_op jit(solution)/shard_map/krs,kqs->krq/dot_general | solution.py:36
  96.9 1.0 copy-done.2
  97.9 0.0 copy-start.3
  97.9 2.9 %fusion = f32[16,32,16]{1,2,0:T(8,128)S(1)} fusion(bf16[2,16,32,4096]{3,2,1,0:T(8,128)(2,1)S(1)} %copy-done.2, bf16[2,16,16,4096]{3,2,1,0:T(8,128)(2,1)} %all-gather.2.cloned.1.call-done), kind=kOutput, calls=%fused_computation | convolution fusion | flops 67108864 | bytes 6324224 | tf_op jit(solution)/shard_map/krs,kqs->krq/dot_general | solution.py:42
  100.8 0.0 copy-done.3
  100.8 1.2 fusion.20
  102.1 1.2 fusion.26
  103.3 0.0 copy-start
  103.3 0.0 copy-start.1
  103.3 0.5 copy.9
  103.8 0.9 reshape.10
  104.7 16.5 %all-to-all-start = ((f32[16,1,1024]{2,1,0:T(1,128)}), f32[16,1,1024]{2,1,0:T(1,128)S(1)}, u32[]{:S(2)}, u32[]{:S(2)}) async-start(f32[16,1,1024]{2,1,0:T(1,128)} %reshape.10), calls=%async_computation | async-start | bytes 131072 | tf_op jit(solution)/shard_map/all_to_all | solution.py:47
  121.1 4.1 %negate_multiply_fusion = (f32[256,1024]{1,0:T(8,128)S(1)}, f32[256,1024]{1,0:T(8,128)S(1)}) fusion(), kind=kLoop, calls=%fused_computation.30 | loop fusion | flops 4456448 | bytes 2097152 | tf_op jit(solution)/shard_map/mul | solution.py:16
  125.3 3.2 %all-to-all-done = f32[16,1,1024]{2,1,0:T(1,128)S(1)} async-done(((f32[16,1,1024]{2,1,0:T(1,128)}), f32[16,1,1024]{2,1,0:T(1,128)S(1)}, u32[]{:S(2)}, u32[]{:S(2)}) %all-to-all-start) | async-done | bytes 65568 | tf_op jit(solution)/shard_map/all_to_all | solution.py:47
  128.5 0.5 broadcast.20
  129.0 0.8 reduce
  129.8 0.2 reshape.11
  130.0 0.4 copy.11
  130.4 0.3 reshape.8
  130.7 0.0 copy-done
  130.7 0.0 copy-done.1
  130.7 1.3 fusion.16
  132.0 0.8 copy.12
  (1 shorter events, 0.0 us)
Async XLA Ops:
  6.5 86.1 %all-gather.2.cloned.1.call-start = ((), (), s32[]{:S(2)}) async-start(), calls=%async_computation.1 | async-start | bytes 4456448 | tf_op jit(solution)/shard_map/all_gather | solution.py:32
  92.7 5.2 %copy-start.2 = (bf16[2,16,32,4096]{3,2,1,0:T(8,128)(2,1)S(1)}, bf16[2,16,32,4096]{3,2,1,0:T(8,128)(2,1)}, u32[]{:S(2)}) copy-start(bf16[2,16,32,4096]{3,2,1,0:T(8,128)(2,1)} %param.4) | copy-start | bytes 25165828
  97.9 2.9 %copy-start.3 = (bf16[2,16,16,4096]{3,2,1,0:T(8,128)(2,1)S(1)}, bf16[2,16,16,4096]{3,2,1,0:T(8,128)(2,1)}, u32[]{:S(2)}) copy-start(bf16[2,16,16,4096]{3,2,1,0:T(8,128)(2,1)} %all-gather.2.cloned.1.call-done) | copy-start | bytes 12582916
  103.3 27.4 %copy-start = (s32[16,2]{0,1:T(2,128)S(1)}, s32[16,2]{0,1:T(2,128)}, u32[]{:S(2)}) copy-start(s32[16,2]{0,1:T(2,128)} %param.7) | copy-start | bytes 388
  103.3 27.4 %copy-start.1 = (s32[16,2]{0,1:T(2,128)S(1)}, s32[16,2]{0,1:T(2,128)}, u32[]{:S(2)}) copy-start(s32[16,2]{0,1:T(2,128)} %param.6) | copy-start | bytes 388
  104.7 23.8 %all-to-all-start = ((f32[16,1,1024]{2,1,0:T(1,128)}), f32[16,1,1024]{2,1,0:T(1,128)S(1)}, u32[]{:S(2)}, u32[]{:S(2)}) async-start(f32[16,1,1024]{2,1,0:T(1,128)} %reshape.10), calls=%async_computation | async-start | bytes 131072 | tf_op jit(solution)/shard_map/all_to_all | solution.py:47
Sparse Core Ops, SparseCore 0:
  9.1 83.5 all-gather.1
where the time goes:
time: 140 us
  waiting for transfers between devices  87.5 us (62%)
  starting transfers between devices  16.5 us (12%)
  between operations  13.5 us (10%)
  matrix products  10.9 us (8%)
  other arithmetic  6.75 us (5%)
  local copies, waits for them, and re-layouts  4.55 us (3%)
    all_gather x1, waiting for transfers between devices, per_device(): gathered = lax.all_gather(focus_half, 'recv', axis=3, tiled=True)  84.3 us
    all_to_all x1, starting transfers between devices, per_device(): lax.all_to_all(spectra, 'freq', split_axis=2, concat_axis=1, tiled=True)  16.5 us
    dot_general x1, matrix products, per_device(): jnp.einsum('krs,kqs->krq', response[1], gathered[1], preferred_element_ty...  4.2 us
    mul x1, other arithmetic, make_table(): return jnp.concatenate([jnp.cos(phase) * scale, -jnp.sin(phase) * scale], 0)  4.15 us
    all_to_all x1, waiting for transfers between devices, per_device(): lax.all_to_all(spectra, 'freq', split_axis=2, concat_axis=1, tiled=True)  3.18 us
    dot_general x1, matrix products, per_device(): jnp.einsum('krs,kqs->krq', response[1], gathered[0], preferred_element_ty...  2.94 us
  transfers between devices with their start and end apart: 2, of which 2 were waited for; matrix products, arithmetic and copies ran while one was open for 3% of the time, Pallas kernels for 0%

commit v1 on v0

--- a/solution.py
+++ b/solution.py
@@ -29,7 +29,8 @@
 def per_device(response, focusing, window_onset, window_end):
     focal = focusing.shape[2]
     focus_half = focusing.astype(jnp.bfloat16)
-    gathered = lax.all_gather(focus_half, "recv", axis=3, tiled=True)
+    sent = jnp.stack([focus_half] * lax.axis_size("recv"))
+    gathered = jnp.concatenate(lax.all_to_all(sent, "recv", 0, 0), axis=3)
     real_part = jnp.einsum(
         "krs,kqs->krq", response[0], gathered[0], preferred_element_type=jnp.float32
     )

time: 140 us -> 150 us (1.071)
  blocking collectives: 0 us -> 102 us
  waiting for transfers between devices: 87.5 us -> 3.16 us
  between operations: 13.5 us -> 0.13 us
  local copies, waits for them, and re-layouts: 4.55 us -> 14.3 us
  starting transfers between devices: 16.5 us -> 9.57 us
  matrix products: 10.9 us -> 13.8 us
    all_to_all x0 -> x1, blocking collectives: none -> 102 us  [per_device(): gathered = jnp.concatenate(lax.all_to_all(sent, 'recv', 0, 0), axis=3)]
    all_gather x1 -> x0, waiting for transfers between devices: 84.3 us -> none  [per_device(): gathered = lax.all_gather(focus_half, 'recv', axis=3, tiled=True)]
    all_to_all x1, starting transfers between devices: 16.5 us -> 9.57 us  [per_device(): lax.all_to_all(spectra, 'freq', split_axis=2, concat_axis=1, tiled=True)]
    slice x0 -> x3, local copies, waits for them, and re-layouts: none -> 5.6 us  [the longest x2 2.84 us: per_device(): gathered[1]]
    squeeze x0 -> x2, local copies, waits for them, and re-layouts: none -> 4.69 us  [the longest x1 2.35 us: per_device(): gathered[0]]
    dot_general x1, matrix products: 1.22 us -> 3.57 us  [per_device(): jnp.einsum('krs,kqs->krq', response[0], gathered[0], preferred_element_ty...]
  transfers between devices with their start and end apart: 2 -> 1, of which waited for: 2 -> 1; matrix products, arithmetic and copies ran while one was open for 3% -> 3% of each run, Pallas kernels for 0% -> 0%
where the time goes in v1:
time: 150 us; the launch traced here: 149 us
  blocking collectives  102 us (68%)
  local copies, waits for them, and re-layouts  14.3 us (10%)
  matrix products  13.8 us (9%)
  starting transfers between devices  9.57 us (6%)
  other arithmetic  6.05 us (4%)
  waiting for transfers between devices  3.16 us (2%)
    all_to_all x1, blocking collectives, per_device(): gathered = jnp.concatenate(lax.all_to_all(sent, 'recv', 0, 0), axis=3)  102 us
    all_to_all x1, starting transfers between devices, per_device(): lax.all_to_all(spectra, 'freq', split_axis=2, concat_axis=1, tiled=True)  9.57 us
    dot_general x1, matrix products, per_device(): jnp.einsum('krs,kqs->krq', response[1], gathered[1], preferred_element_ty...  4.2 us
    mul x1, other arithmetic, make_table(): return jnp.concatenate([jnp.cos(phase) * scale, -jnp.sin(phase) * scale], 0)  4.15 us
    dot_general x1, matrix products, per_device(): jnp.einsum('krs,kqs->krq', response[0], gathered[0], preferred_element_ty...  3.57 us
    dot_general x1, matrix products, per_device(): jnp.einsum('krs,kqs->krq', response[1], gathered[0], preferred_element_ty...  3.56 us
    all_to_all x1, waiting for transfers between devices, per_device(): lax.all_to_all(spectra, 'freq', split_axis=2, concat_axis=1, tiled=True)  3.16 us
  transfers between devices with their start and end apart: 1, of which 1 were waited for; matrix products, arithmetic and copies ran while one was open for 3% of the time, Pallas kernels for 0%

profile of v1, /device:TPU:1, one launch (start us, length us, event | category | flops | bytes accessed | tf_op | source)
XLA Modules:
  0.0 149.3 jit_solution(13537201095776670759)
XLA Ops:
  0.0 1.1 convert_element_type.8
  1.1 0.5 stack.8
  1.5 102.3 %all_to_all.20 = bf16[16,2,16,16,256]{4,3,2,1,0:T(8,128)(2,1)S(1)} all-to-all(bf16[16,2,16,16,256]{4,3,2,1,0:T(8,128)(2,1)S(1)} %stack.8), channel_id=1, replica_groups=mesh['freq'=16,'recv'=16] {'recv'}, dimensions={0} | all-to-all | bytes 8388608 | tf_op jit(solution)/shard_map/all_to_all | solution.py:33
  103.9 1.6 %fusion.37 = (bf16[1,16,16,16,256]{4,2,1,0,3:T(8,128)(2,1)S(1)}, bf16[1,16,16,16,256]{4,2,1,0,3:T(8,128)(2,1)}) fusion(bf16[2,16,16,16,256]{4,2,1,0,3:T(8,128)(2,1)S(1)} %bitcast.55), kind=kLoop, calls=%fused_computation.38 | loop fusion | bytes 8388608 | tf_op jit(solution)/shard_map/slice | solution.py:38
  105.5 1.2 copy.10
  106.7 2.3 %squeeze.19 = bf16[16,16,4096]{2,1,0:T(8,128)(2,1)} reshape(bf16[1,16,16,16,256]{4,3,2,1,0:T(8,128)(2,1)S(1)} %copy.10) | data formatting | bytes 4194304 | tf_op jit(solution)/shard_map/squeeze | solution.py:38
  109.0 2.8 %copy.9 = bf16[1,16,16,16,256]{4,3,2,1,0:T(8,128)(2,1)S(1)} copy(bf16[1,16,16,16,256]{4,2,1,0,3:T(8,128)(2,1)} %get-tuple-element.6) | data formatting | bytes 4194304 | tf_op jit(solution)/shard_map/slice | solution.py:35
  111.8 2.3 %squeeze.17 = bf16[16,16,4096]{2,1,0:T(8,128)(2,1)} reshape(bf16[1,16,16,16,256]{4,3,2,1,0:T(8,128)(2,1)S(1)} %copy.9) | data formatting | bytes 4194304 | tf_op jit(solution)/shard_map/squeeze | solution.py:35
  114.1 0.0 copy-start.1
  114.2 0.0 slice-start
  114.2 4.2 %fusion.2 = f32[16,32,16]{1,2,0:T(8,128)S(1)} fusion(bf16[16,16,4096]{2,1,0:T(8,128)(2,1)} %squeeze.19, bf16[2,16,32,4096]{3,2,1,0:T(8,128)(2,1)} %param.4), kind=kOutput, calls=%fused_computation.2 | convolution fusion | flops 67108864 | bytes 6324224 | tf_op jit(solution)/shard_map/krs,kqs->krq/dot_general | solution.py:37
  118.4 0.0 copy-done.1
  118.4 0.0 slice-start.1
  118.4 3.6 %fusion = f32[16,32,16]{1,2,0:T(8,128)S(1)} fusion(bf16[16,16,4096]{2,1,0:T(8,128)(2,1)S(1)} %copy-done.1, bf16[2,16,32,4096]{3,2,1,0:T(8,128)(2,1)} %param.4), kind=kOutput, calls=%fused_computation | convolution fusion | flops 67108864 | bytes 6324224 | tf_op jit(solution)/shard_map/krs,kqs->krq/dot_general | solution.py:43
  121.9 0.0 copy-start
  121.9 3.6 %fusion.20 = f32[1,16,32,16]{2,3,1,0:T(8,128)S(1)} fusion(f32[16,32,16]{1,2,0:T(8,128)S(1)} %fusion.2, bf16[16,16,4096]{2,1,0:T(8,128)(2,1)S(1)} %copy-done.1, bf16[2,16,32,4096]{3,2,1,0:T(8,128)(2,1)} %param.4), kind=kOutput, calls=%fused_computation.22 | convolution fusion | flops 67117056 | bytes 6356992 | tf_op jit(solution)/shard_map/krs,kqs->krq/dot_general | solution.py:34
  125.5 0.0 slice-done
  125.5 0.0 slice-done.1
  125.5 0.0 copy-done
  125.5 1.2 fusion.26
  126.8 0.5 copy.11
  127.2 0.9 reshape.21
  128.1 9.6 %all-to-all-start.1 = ((f32[16,1,1024]{2,1,0:T(1,128)}), f32[16,1,1024]{2,1,0:T(1,128)S(1)}, u32[]{:S(2)}, u32[]{:S(2)}) async-start(f32[16,1,1024]{2,1,0:T(1,128)} %reshape.21), calls=%async_computation.1 | async-start | bytes 131072 | tf_op jit(solution)/shard_map/all_to_all | solution.py:48
  137.7 0.0 copy-start.2
  137.7 0.0 copy-start.3
  137.7 4.1 %negate_multiply_fusion = (f32[256,1024]{1,0:T(8,128)S(1)}, f32[256,1024]{1,0:T(8,128)S(1)}) fusion(), kind=kLoop, calls=%fused_computation.28 | loop fusion | flops 4456448 | bytes 2097152 | tf_op jit(solution)/shard_map/mul | solution.py:16
  141.9 3.2 %all-to-all-done.1 = f32[16,1,1024]{2,1,0:T(1,128)S(1)} async-done(((f32[16,1,1024]{2,1,0:T(1,128)}), f32[16,1,1024]{2,1,0:T(1,128)S(1)}, u32[]{:S(2)}, u32[]{:S(2)}) %all-to-all-start.1) | async-done | bytes 65568 | tf_op jit(solution)/shard_map/all_to_all | solution.py:48
  145.0 0.5 broadcast.22
  145.5 0.8 reduce
  146.3 0.2 reshape.22
  146.5 0.4 copy.13
  147.0 0.3 reshape.19
  147.3 0.0 copy-done.2
  147.3 0.0 copy-done.3
  147.3 1.3 fusion.16
  148.6 0.8 copy.14
  (2 shorter events, 0.0 us)
Async XLA Ops:
  114.1 4.2 %copy-start.1 = (bf16[16,16,4096]{2,1,0:T(8,128)(2,1)S(1)}, bf16[16,16,4096]{2,1,0:T(8,128)(2,1)}, u32[]{:S(2)}) copy-start(bf16[16,16,4096]{2,1,0:T(8,128)(2,1)} %squeeze.17) | copy-start | bytes 6291460
  114.2 11.3 %slice-start = ((s8[8388608]{0:T(1024)(128)(4,1)}), s8[4194304]{0:T(1024)(128)(4,1)S(1)}, s32[]{:S(2)}) async-start(s8[8388608]{0:T(1024)(128)(4,1)} %bitcast.59), calls=%async_computation.2 | async-start | bytes 8388608
  118.4 7.1 %slice-start.1 = ((s8[8388608]{0:T(1024)(128)(4,1)}), s8[4194304]{0:T(1024)(128)(4,1)S(1)}, s32[]{:S(2)}) async-start(s8[8388608]{0:T(1024)(128)(4,1)} %bitcast.59), calls=%async_computation.3 | async-start | bytes 8388608
  121.9 3.6 %copy-start = (bf16[16,16,4096]{2,1,0:T(8,128)(2,1)S(1)}, bf16[16,16,4096]{2,1,0:T(8,128)(2,1)}, u32[]{:S(2)}) copy-start(bf16[16,16,4096]{2,1,0:T(8,128)(2,1)} %squeeze.19) | copy-start | bytes 6291460
  128.1 16.9 %all-to-all-start.1 = ((f32[16,1,1024]{2,1,0:T(1,128)}), f32[16,1,1024]{2,1,0:T(1,128)S(1)}, u32[]{:S(2)}, u32[]{:S(2)}) async-start(f32[16,1,1024]{2,1,0:T(1,128)} %reshape.21), calls=%async_computation.1 | async-start | bytes 131072 | tf_op jit(solution)/shard_map/all_to_all | solution.py:48
  137.7 9.6 %copy-start.2 = (s32[16,2]{0,1:T(2,128)S(1)}, s32[16,2]{0,1:T(2,128)}, u32[]{:S(2)}) copy-start(s32[16,2]{0,1:T(2,128)} %param.7) | copy-start | bytes 388
  137.7 9.6 %copy-start.3 = (s32[16,2]{0,1:T(2,128)S(1)}, s32[16,2]{0,1:T(2,128)}, u32[]{:S(2)}) copy-start(s32[16,2]{0,1:T(2,128)} %param.6) | copy-start | bytes 388
